TPU v7x, 128 devices: a whole 4x4x4 slice. The times are simulated.
128 devices in a mesh: side: 2 (over core), grp: 64 (over x, y, z).
Axes of the slice: x: 4, y: 4, z: 4, core: 2. Of those that a mesh axis runs over, the one named last changes fastest.
Arguments:
- poles: float32 [65536], P(('side', 'grp')), may hold values from 0 to 1, as said below
- coupling: float32 [65536], P(('side', 'grp')), may hold values from -0.0234375 to 0.0234375
- kinds: int32 [65536], P(('side', 'grp')), may hold values from 0 to 3
- permutation: int32 [2, 32768], P('side'), may hold values from 0 to 32767, each once within a row
- block_map: int32 [2, 64, 2, 128], P('side', 'grp'), may hold values from 0 to 1, as said below
- left_vectors: bfloat16 [2, 12288, 32768], P('side', 'grp'), may hold values from -6 to 6
- right_vectors: bfloat16 [2, 12288, 32768], P('side', 'grp'), may hold values from -6 to 6
Outputs:
- new_left: bfloat16 [2, 12288, 256], P('side', 'grp')
- new_right: bfloat16 [2, 12288, 256], P('side', 'grp')
- root_offsets: float32 [256], replicated
Inputs may be any that keep to these rules, and one draw needn't show every extreme that they name: Positive; the squares of any two poles differ by at least 0.4 / 65536; for every panel root r, pole_sq[r] < pole_sq[r + 1] and no pole's square lies strictly between them. `block_map`: each row of the last dimension (one child, row block and matrix) has at most 64 ones; some row has exactly 64. A zero marks a block whose entries are ignored.
All inputs are finite; a program needn't handle non-finite values.
Results may differ from a plain program's by a relative error of at most 0.008.
Values may be sent and summed in bfloat16 or wider, within the bound.
A program may use at most 192 MiB of HBM per device.

v0:
```python
import jax
import jax.numpy as jnp
from jax import lax
from jax.sharding import PartitionSpec as P

P_SIZE = 128
BW = 256
ITERS = 8


def inverse_sums(pole_sq, lead_weight, tail_weight, shifts, exponent):
    pole_count = pole_sq.shape[0]
    step_len = min(4096, pole_count)
    blocks = pole_count // step_len

    def visit_block(running, block_items):
        sq_block, lead_block, tail_block = block_items
        inverse = 1.0 / (sq_block[:, None] - shifts[None, :])
        leading = inverse if exponent == 1 else inverse * inverse
        return (
            (
                running[0] + jnp.sum(lead_block[:, None] * leading, 0),
                running[1] + jnp.sum(tail_block[:, None] * inverse * inverse, 0),
            ),
            None,
        )

    initial = (jnp.zeros(shifts.shape, jnp.float32), jnp.zeros(shifts.shape, jnp.float32))
    block_items = (
        pole_sq.reshape(blocks, step_len),
        lead_weight.reshape(blocks, step_len),
        tail_weight.reshape(blocks, step_len),
    )
    totals, _ = lax.scan(visit_block, initial, block_items)
    return totals


def apply_blocks(vectors, placed, block_flags):
    keep_mask = jnp.repeat(block_flags, BW).astype(jnp.bfloat16)
    return jnp.dot(vectors, placed * keep_mask[:, None], preferred_element_type=jnp.float32)


def on_device(poles, coupling, kinds, permutation, block_map, left_vectors, right_vectors):
    own_count = poles.shape[0]
    side_count = lax.axis_size("side")
    group_count = lax.axis_size("grp")
    half_poles = own_count * group_count
    total_poles = half_poles * side_count
    root_total = 2 * P_SIZE
    pole_sq = poles * poles
    alive = (kinds != 0).astype(jnp.float32)
    in_left = ((kinds == 1) | (kinds == 2)).astype(jnp.float32)
    in_right = ((kinds == 2) | (kinds == 3)).astype(jnp.float32)
    weight = alive * coupling * coupling
    u_weight = in_left * coupling * coupling
    v_weight = in_right * pole_sq * coupling * coupling
    coef_u = in_left * coupling
    coef_v = in_right * poles * coupling
    ranks = jnp.arange(P_SIZE, dtype=jnp.int32)
    root_index = jnp.concatenate([half_poles - P_SIZE + ranks, total_poles - 2 * P_SIZE + ranks])
    offset = (lax.axis_index("side") * group_count + lax.axis_index("grp")) * own_count

    def pick_pole(global_index):
        local_index = global_index - offset
        inside = (local_index >= 0) & (local_index < own_count)
        return jnp.where(inside, pole_sq[jnp.clip(local_index, 0, own_count - 1)], 0.0)

    lower_pole, upper_pole = lax.psum(
        (pick_pole(root_index), pick_pole(root_index + 1)), ("side", "grp")
    )
    pole_gap = upper_pole - lower_pole
    low_bound = lower_pole + 0.1 * pole_gap
    high_bound = upper_pole - 0.1 * pole_gap
    shifts = lower_pole + 0.5 * pole_gap
    for step in range(ITERS):
        own_value, own_slope = inverse_sums(pole_sq, weight, weight, shifts, 1)
        sum_value, slope_value = lax.psum((own_value, own_slope), ("side", "grp"))
        secular_value = 1.0 + sum_value
        shifts = jnp.clip(shifts - 0.5 * secular_value / slope_value, low_bound, high_bound)
    root_offsets = (shifts - lower_pole) / pole_gap
    own_u, own_v = inverse_sums(pole_sq, u_weight, v_weight, shifts, 2)
    sum_u, sum_v = lax.psum((own_u, own_v), ("side", "grp"))
    norm_u = jnp.sqrt(sum_u)
    norm_v = jnp.sqrt(1.0 + sum_v)
    placing = permutation[0]
    inverse = 1.0 / (pole_sq[:, None] - shifts[None, :])
    rows_u = (coef_u[:, None] * inverse / norm_u[None, :]).astype(jnp.bfloat16)
    rows_v = (coef_v[:, None] * inverse / norm_v[None, :]).astype(jnp.bfloat16)
    child_u, child_v = (
        lax.all_gather(rows_u, "grp", axis=0, tiled=True),
        lax.all_gather(rows_v, "grp", axis=0, tiled=True),
    )
    placed_u = jnp.zeros((half_poles, root_total), jnp.bfloat16).at[placing].set(child_u)
    placed_v = jnp.zeros((half_poles, root_total), jnp.bfloat16).at[placing].set(child_v)
    new_left = apply_blocks(left_vectors[0], placed_u, block_map[0, 0, 0]).astype(jnp.bfloat16)
    new_right = apply_blocks(right_vectors[0], placed_v, block_map[0, 0, 1]).astype(jnp.bfloat16)
    return (new_left[None], new_right[None], root_offsets)


def solution(mesh):
    return jax.shard_map(
        on_device,
        mesh=mesh,
        in_specs=(
            P(("side", "grp")),
            P(("side", "grp")),
            P(("side", "grp")),
            P("side", None),
            P("side", "grp", None, None),
            P("side", "grp", None),
            P("side", "grp", None),
        ),
        out_specs=(P("side", "grp", None), P("side", "grp", None), P()),
        check_vma=False,
    )
```

profile of v0, /device:TPU:1, one launch (start us, length us, event | category | flops | bytes accessed | tf_op | source)
XLA Modules:
  0.0 1097.9 jit_solution(6579606501836008609)
XLA Ops:
  7.2 0.7 or_select_fusion
  8.0 0.7 multiply_multiply_fusion.9
  8.7 1.9 gather_fusion
  10.7 1.9 gather_fusion.1
  12.6 68.7 %all-reduce.9 = (f32[256]{0:T(256)S(1)}, f32[256]{0:T(256)S(1)}) all-reduce(f32[256]{0:T(256)S(1)} %get-tuple-element.369, f32[256]{0:T(256)S(1)} %get-tuple-element.368), channel_id=1, replica_groups=mesh['side'=2,'grp'=64] {'side','grp'}, use_global_device_ids=true, to_apply=%region_0.1 | all-reduce | flops 512 | bytes 4096 | tf_op jit(solution)/shard_map/psum | solution.py:68
  81.5 62.6 %all-reduce.8 = (f32[256]{0:T(256)S(1)}, f32[256]{0:T(256)S(1)}) all-reduce(f32[256]{0:T(256)S(1)} %get-tuple-element.327, f32[256]{0:T(256)S(1)} %get-tuple-element.326), channel_id=1, replica_groups=mesh['side'=2,'grp'=64] {'side','grp'}, use_global_device_ids=true, to_apply=%region_5.6 | all-reduce | flops 512 | bytes 4096 | tf_op jit(solution)/shard_map/psum | solution.py:77
  144.2 0.2 multiply_reduce_fusion.6
  144.4 64.1 %all-reduce.7 = (f32[256]{0:T(256)S(1)}, f32[256]{0:T(256)S(1)}) all-reduce(f32[256]{0:T(256)S(1)} %get-tuple-element.325, f32[256]{0:T(256)S(1)} %get-tuple-element.324), channel_id=1, replica_groups=mesh['side'=2,'grp'=64] {'side','grp'}, use_global_device_ids=true, to_apply=%region_9.10 | all-reduce | flops 512 | bytes 4096 | tf_op jit(solution)/shard_map/psum | solution.py:77
  208.5 0.2 multiply_reduce_fusion.5
  208.8 62.5 %all-reduce.6 = (f32[256]{0:T(256)S(1)}, f32[256]{0:T(256)S(1)}) all-reduce(f32[256]{0:T(256)S(1)} %get-tuple-element.323, f32[256]{0:T(256)S(1)} %get-tuple-element.322), channel_id=1, replica_groups=mesh['side'=2,'grp'=64] {'side','grp'}, use_global_device_ids=true, to_apply=%region_13.14 | all-reduce | flops 512 | bytes 4096 | tf_op jit(solution)/shard_map/psum | solution.py:77
  271.3 0.2 multiply_reduce_fusion.4
  271.5 64.0 %all-reduce.5 = (f32[256]{0:T(256)S(1)}, f32[256]{0:T(256)S(1)}) all-reduce(f32[256]{0:T(256)S(1)} %get-tuple-element.321, f32[256]{0:T(256)S(1)} %get-tuple-element.320), channel_id=1, replica_groups=mesh['side'=2,'grp'=64] {'side','grp'}, use_global_device_ids=true, to_apply=%region_17.18 | all-reduce | flops 512 | bytes 4096 | tf_op jit(solution)/shard_map/psum | solution.py:77
  335.6 0.2 multiply_reduce_fusion.3
  335.8 62.5 %all-reduce.4 = (f32[256]{0:T(256)S(1)}, f32[256]{0:T(256)S(1)}) all-reduce(f32[256]{0:T(256)S(1)} %get-tuple-element.319, f32[256]{0:T(256)S(1)} %get-tuple-element.318), channel_id=1, replica_groups=mesh['side'=2,'grp'=64] {'side','grp'}, use_global_device_ids=true, to_apply=%region_21.22 | all-reduce | flops 512 | bytes 4096 | tf_op jit(solution)/shard_map/psum | solution.py:77
  398.3 0.2 multiply_reduce_fusion.2
  398.5 64.0 %all-reduce.3 = (f32[256]{0:T(256)S(1)}, f32[256]{0:T(256)S(1)}) all-reduce(f32[256]{0:T(256)S(1)} %get-tuple-element.317, f32[256]{0:T(256)S(1)} %get-tuple-element.316), channel_id=1, replica_groups=mesh['side'=2,'grp'=64] {'side','grp'}, use_global_device_ids=true, to_apply=%region_25.26 | all-reduce | flops 512 | bytes 4096 | tf_op jit(solution)/shard_map/psum | solution.py:77
  462.6 0.2 multiply_reduce_fusion.1
  462.8 62.5 %all-reduce.2 = (f32[256]{0:T(256)S(1)}, f32[256]{0:T(256)S(1)}) all-reduce(f32[256]{0:T(256)S(1)} %get-tuple-element.315, f32[256]{0:T(256)S(1)} %get-tuple-element.314), channel_id=1, replica_groups=mesh['side'=2,'grp'=64] {'side','grp'}, use_global_device_ids=true, to_apply=%region_29.30 | all-reduce | flops 512 | bytes 4096 | tf_op jit(solution)/shard_map/psum | solution.py:77
  525.3 0.2 multiply_reduce_fusion
  525.6 64.5 %all-reduce.1 = (f32[256]{0:T(256)S(1)}, f32[256]{0:T(256)S(1)}) all-reduce(f32[256]{0:T(256)S(1)} %get-tuple-element.313, f32[256]{0:T(256)S(1)} %get-tuple-element.312), channel_id=1, replica_groups=mesh['side'=2,'grp'=64] {'side','grp'}, use_global_device_ids=true, to_apply=%region_33.34 | all-reduce | flops 512 | bytes 4096 | tf_op jit(solution)/shard_map/psum | solution.py:77
  590.1 0.6 subtract_divide_fusion.9
  590.6 0.3 fusion.40
  590.9 62.5 %all-reduce = (f32[256]{0:T(256)S(1)}, f32[256]{0:T(256)S(1)}) all-reduce(f32[256]{0:T(256)S(1)} %get-tuple-element.329, f32[256]{0:T(256)S(1)} %get-tuple-element.328), channel_id=1, replica_groups=mesh['side'=2,'grp'=64] {'side','grp'}, use_global_device_ids=true, to_apply=%region_35.36 | all-reduce | flops 512 | bytes 4096 | tf_op jit(solution)/shard_map/psum | solution.py:82
  653.5 1.1 divide_convert_fusion
  654.6 0.7 all-gather.3.cloned.1.call-update
  655.3 0.7 convert.4
  656.2 1.0 compare_select_fusion
  657.3 98.9 %all-gather.5.cloned.1.call-done = bf16[32768,256]{1,0:T(8,128)(2,1)} async-done(((bf16[512,256]{1,0:T(8,128)(2,1)}), bf16[32768,256]{1,0:T(8,128)(2,1)}) %all-gather.5.cloned.1.call-update) | async-done | bytes 16777232 | tf_op jit(solution)/shard_map/all_gather | solution.py:91
  756.2 146.8 %scatter_custom_fusion.1 = bf16[32768,256]{1,0:T(8,128)(2,1)} fusion(s32[32768]{0:T(1024)S(1)} %bitcast.41, bf16[32768,256]{1,0:T(8,128)(2,1)} %all-gather.5.cloned.1.call-done, bf16[]{:T(256)} %constant.164.clone.1), kind=kCustom, calls=%fused_computation.12 | custom fusion | bytes 16777728 | tf_op jit(solution)/shard_map/scatter | solution.py:94
  903.0 20.5 %fusion.22 = bf16[1,192,256]{2,1,0:T(8,128)(2,1)} fusion(bf16[32768,256]{1,0:T(8,128)(2,1)} %scatter_custom_fusion.1, bf16[32768]{0:T(1024)(128)(2,1)S(1)} %bitcast.44, bf16[1,192,32768]{2,1,0:T(8,128)(2,1)} %param.13), kind=kOutput, calls=%fused_computation.18 | convolution fusion | flops 3229663232 | bytes 29523968 | tf_op jit(solution)/shard_map/dot_general | solution.py:40
  923.5 146.8 %scatter_custom_fusion = bf16[32768,256]{1,0:T(8,128)(2,1)} fusion(s32[32768]{0:T(1024)S(1)} %bitcast.42, bf16[32768,256]{1,0:T(8,128)(2,1)} %all-gather.3.cloned.1.call-done, bf16[]{:T(256)} %constant.164.clone.1), kind=kCustom, calls=%fused_computation.14 | custom fusion | bytes 16777728 | tf_op jit(solution)/shard_map/scatter | solution.py:93
  1070.4 20.5 %fusion.27 = bf16[1,192,256]{2,1,0:T(8,128)(2,1)} fusion(bf16[32768,256]{1,0:T(8,128)(2,1)} %scatter_custom_fusion, bf16[32768]{0:T(1024)(128)(2,1)S(1)} %bitcast.43, bf16[1,192,32768]{2,1,0:T(8,128)(2,1)} %param.12), kind=kOutput, calls=%fused_computation.19 | convolution fusion | flops 3229663232 | bytes 29523968 | tf_op jit(solution)/shard_map/dot_general | solution.py:40
  (25 shorter events, 0.6 us)
Async XLA Ops:
  7.2 749.1 %all-gather.5.cloned.1.call-start = ((), (), s32[]{:S(2)}) async-start(), calls=%async_computation.1 | async-start | bytes 17039360 | tf_op jit(solution)/shard_map/all_gather | solution.py:91
  654.6 268.9 %all-gather.3.cloned.1.call-start = ((), (), s32[]{:S(2)}) async-start(), calls=%async_computation | async-start | bytes 17039360 | tf_op jit(solution)/shard_map/all_gather | solution.py:90
Sparse Core Ops, SparseCore 0:
  654.7 101.4 all-gather.4
  759.1 103.9 all-gather.2
where the time goes:
time: 1110 us; the launch traced here: 1100 us
  blocking collectives  638 us (57%)
  local copies, waits for them, and re-layouts  298 us (27%)
  waiting for transfers between devices  99.7 us (9%)
  matrix products  41 us (4%)
  between operations  14.4 us (1%)
    psum x8, blocking collectives, on_device(): sum_value, slope_value = lax.psum((own_value, own_slope), ('side', 'grp'))  507 us
    scatter x1, local copies, waits for them, and re-layouts, on_device(): jnp.zeros((half_poles, root_total), jnp.bfloat16).at[placing].set(child_u)  147 us
    scatter x1, local copies, waits for them, and re-layouts, on_device(): jnp.zeros((half_poles, root_total), jnp.bfloat16).at[placing].set(child_v)  147 us
    all_gather x1, waiting for transfers between devices, on_device(): lax.all_gather(rows_v, 'grp', axis=0, tiled=True)  98.9 us
    psum x1, blocking collectives, on_device(): lax.psum((pick_pole(root_index), pick_pole(root_index + 1)), ('side', 'gr...  68.7 us
    psum x1, blocking collectives, on_device(): sum_u, sum_v = lax.psum((own_u, own_v), ('side', 'grp'))  62.5 us
    dot_general x2, matrix products, apply_blocks(): jnp.dot(vectors, placed * keep_mask[:, None], preferred_element_type=jnp....  41 us
  transfers between devices with their start and end apart: 2, of which 1 were waited for; matrix products, arithmetic and copies ran while one was open for 15% of the time, Pallas kernels for 0%

commit v1 on v0

v1 whole, which is shorter than its diff:
```python
import functools

import jax
import jax.numpy as jnp
from jax import lax
from jax.experimental import pallas as pl
from jax.experimental.pallas import tpu as pltpu
from jax.sharding import PartitionSpec as P

MESH = pl.DeviceIdType.MESH
ITERS = 8
LANES = 128
BW = 256
CHUNK = 4096
F32 = jnp.float32
BF16 = jnp.bfloat16


def far_first(i):
    return (2 + i + i // 2 + 2 * (i // 3)) % 4


def chip_at(grp, i):
    x = (grp // 16 + far_first(i // 16)) % 4
    y = (grp // 4 + far_first((i // 4) % 4)) % 4
    z = (grp + far_first(i % 4)) % 4
    return x * 16 + y * 4 + z


def recip(value):
    guess = pl.reciprocal(value, approx=True)
    return guess + guess * (1.0 - value * guess)


def total(value):
    return jnp.sum(value, axis=(0, 1), keepdims=True)


def merge_kernel(
    poles_ref, coupling_ref, kinds_ref, perm_ref, map_ref, left_ref, right_ref,
    out_left, out_right, out_offsets,
    held, raw, one_hot, pieces, spread, found, placed, sq, weight, answers,
    shift_cols, cauchy_a, cauchy_b, acc, load_sem, send_sem, recv_sem,
):
    side = lax.axis_index("side")
    grp = lax.axis_index("grp")
    me = side * 64 + grp
    rows = left_ref.shape[0]
    count = left_ref.shape[1]
    groups = raw.shape[1]

    loads = [
        pltpu.make_async_copy(left_ref, held.at[pl.ds(0, rows)], load_sem.at[0]),
        pltpu.make_async_copy(right_ref, held.at[pl.ds(rows, rows)], load_sem.at[1]),
    ]
    for load in loads:
        load.start()

    barrier = pltpu.get_barrier_semaphore()

    def greet(i, _):
        other = (me + 1 + i) % 128
        pl.semaphore_signal(barrier, inc=1, device_id=(other // 64, other % 64), device_id_type=MESH)
        return 0

    lax.fori_loop(0, 127, greet, 0)

    raw[side, grp, 0] = poles_ref[...]
    raw[side, grp, 1] = coupling_ref[...]
    raw[side, grp, 2] = kinds_ref[...].astype(F32)
    low_digit = lax.broadcasted_iota(jnp.int32, (LANES, LANES), 0)

    def mark(r, _):
        own = perm_ref[pl.ds(r, 1), :] % LANES
        columns = pl.ds(pl.multiple_of(r * LANES, LANES), LANES)
        one_hot[:, columns] = jnp.where(own == low_digit, 1.0, 0.0).astype(BF16)
        return 0

    lax.fori_loop(0, count // LANES, mark, 0, unroll=4)

    pl.semaphore_wait(barrier, 127)

    def send_raw(i, _):
        mine = raw.at[side, grp]
        pltpu.make_async_remote_copy(
            src_ref=mine, dst_ref=mine, send_sem=send_sem.at[0], recv_sem=recv_sem.at[0],
            device_id=(side, chip_at(grp, i)), device_id_type=MESH,
        ).start()
        return 0

    lax.fori_loop(0, 63, send_raw, 0)
    gathered = pltpu.make_async_remote_copy(
        src_ref=raw.at[0, pl.ds(0, 63)], dst_ref=raw.at[0, pl.ds(0, 63)], send_sem=send_sem.at[0],
        recv_sem=recv_sem.at[0], device_id=(1 - side, grp), device_id_type=MESH,
    )
    gathered.wait_recv()

    cross = pltpu.make_async_remote_copy(
        src_ref=raw.at[side], dst_ref=raw.at[side], send_sem=send_sem.at[1], recv_sem=recv_sem.at[1],
        device_id=(1 - side, grp), device_id_type=MESH,
    )
    cross.start()

    def split(j, _):
        pole = raw[side, j, 0]
        coupling = raw[side, j, 1]
        kind = raw[side, j, 2]
        coef_u = jnp.where((kind == 1.0) | (kind == 2.0), coupling, 0.0)
        coef_v = jnp.where(kind >= 2.0, pole * coupling, 0.0)
        square = pole * pole
        high = square.astype(BF16).astype(F32)
        rest = square - high
        middle = rest.astype(BF16).astype(F32)
        u_high = coef_u.astype(BF16).astype(F32)
        v_high = coef_v.astype(BF16).astype(F32)
        for q, piece in enumerate((high, middle, rest - middle, u_high, coef_u - u_high, v_high, coef_v - v_high)):
            pieces[pl.ds(j * 4, 4), q, :] = piece
        return 0

    pieces[:, 7, :] = jnp.zeros_like(pieces[:, 7, :])
    lax.fori_loop(0, groups, split, 0, unroll=2)

    def mask(r, _):
        digit = perm_ref[pl.ds(r, 1), :] // LANES - 4 * grp
        piece = pieces[r]
        columns = pl.ds(pl.multiple_of(r * LANES, LANES), LANES)
        spread[:, columns] = jnp.concatenate(
            [jnp.where(digit == h, piece, 0.0) for h in range(4)], axis=0
        ).astype(BF16)
        return 0

    lax.fori_loop(0, count // LANES, mask, 0, unroll=4)
    found[...] = jnp.zeros_like(found)

    def look_up(i, _):
        columns = pl.ds(pl.multiple_of(i * CHUNK, CHUNK), CHUNK)
        found[...] += lax.dot_general(
            spread[:, columns], one_hot[:, columns], (((1,), (1,)), ((), ())), preferred_element_type=F32
        )
        return 0

    lax.fori_loop(0, count // CHUNK, look_up, 0)
    digits = [found[pl.ds(q, 4, stride=8), :] for q in range(7)]
    placed[grp, 0] = digits[0] + (digits[1] + digits[2])
    placed[grp, 1] = digits[3] + digits[4]
    placed[grp, 2] = digits[5] + digits[6]

    def send_placed(i, _):
        mine = placed.at[grp]
        pltpu.make_async_remote_copy(
            src_ref=mine, dst_ref=mine, send_sem=send_sem.at[2], recv_sem=recv_sem.at[2],
            device_id=(side, chip_at(grp, i)), device_id_type=MESH,
        ).start()
        return 0

    lax.fori_loop(0, 63, send_placed, 0)

    cross.wait_recv()

    def lay_out(j, _):
        pole = jnp.concatenate([raw[0, j, 0], raw[1, j, 0]], axis=0)
        coupling = jnp.concatenate([raw[0, j, 1], raw[1, j, 1]], axis=0)
        kind = jnp.concatenate([raw[0, j, 2], raw[1, j, 2]], axis=0)
        sq[j] = pole * pole
        weight[j] = jnp.where(kind != 0.0, coupling, 0.0) * coupling
        return 0

    lax.fori_loop(0, groups, lay_out, 0, unroll=4)

    lane = lax.broadcasted_iota(jnp.int32, (1, LANES), 1)
    last = groups - 1

    def pick(row, at):
        return total(jnp.where(lane == at, row, 0.0))

    after = jnp.where(me == 127, 0, -1)
    first_low = pick(sq[last, 3:4], me)
    first_high = pick(sq[last, 3:4], me + 1) + pick(sq[0, 4:5], after)
    second_low = pick(sq[last, 6:7], me)
    second_high = pick(sq[last, 6:7], me + 1) + pick(sq[last, 7:8], after)
    lows = (first_low, second_low)
    gaps = (first_high - first_low, second_high - second_low)
    starts = tuple(low + 0.1 * gap for low, gap in zip(lows, gaps))
    ends = tuple(high - 0.1 * gap for high, gap in zip((first_high, second_high), gaps))
    blocks = 8

    def visit(shifts, extra):
        zero = jnp.zeros((8, LANES), F32)
        sums = [[zero, zero], [zero, zero]]
        wide = [jnp.broadcast_to(shift, (8, LANES)) for shift in shifts]
        for b in range(groups // blocks):
            at = pl.ds(b * blocks, blocks)
            sq_block = sq[at]
            lead, tail = extra(at, sq_block)
            for k in range(2):
                inverse = recip(sq_block - wide[k])
                if lead is None:
                    part = tail * inverse
                    sums[k][0] = sums[k][0] + jnp.sum(part, axis=0)
                    sums[k][1] = sums[k][1] + jnp.sum(part * inverse, axis=0)
                else:
                    squared = inverse * inverse
                    sums[k][0] = sums[k][0] + jnp.sum(lead * squared, axis=0)
                    sums[k][1] = sums[k][1] + jnp.sum(tail * squared, axis=0)
        return [[total(s) for s in pair] for pair in sums]

    def step(_, shifts):
        sums = visit(shifts, lambda at, sq_block: (None, weight[at]))
        return tuple(
            jnp.clip(shift - 0.5 * (1.0 + value) / slope, start, end)
            for shift, (value, slope), start, end in zip(shifts, sums, starts, ends)
        )

    shifts = lax.fori_loop(
        0, ITERS, step, tuple(low + 0.5 * gap for low, gap in zip(lows, gaps))
    )

    def norm_weights(at, sq_block):
        kind = jnp.concatenate([raw[0, at, 2], raw[1, at, 2]], axis=1)
        both = weight[at]
        return (
            jnp.where((kind == 1.0) | (kind == 2.0), both, 0.0),
            jnp.where(kind >= 2.0, sq_block * both, 0.0),
        )

    norms = visit(shifts, norm_weights)
    values = [shifts[0], shifts[1]]
    values += [lax.rsqrt(norms[k][0]) for k in range(2)]
    values += [lax.rsqrt(1.0 + norms[k][1]) for k in range(2)]
    values += [(shift - low) / gap for shift, low, gap in zip(shifts, lows, gaps)]
    row = jnp.zeros((1, LANES), F32)
    for k, value in enumerate(values):
        row = jnp.where(lane == k, value, row)
    answers[me] = row

    def send_answer(i, _):
        mine = answers.at[me]
        pltpu.make_async_remote_copy(
            src_ref=mine, dst_ref=mine, send_sem=send_sem.at[3], recv_sem=recv_sem.at[3],
            device_id=((side + i) % 2, chip_at(grp, i // 2)), device_id_type=MESH,
        ).start()
        return 0

    lax.fori_loop(0, 126, send_answer, 0)
    mine = answers.at[me]
    pltpu.make_async_remote_copy(
        src_ref=mine, dst_ref=mine, send_sem=send_sem.at[3], recv_sem=recv_sem.at[3],
        device_id=(1 - side, grp), device_id_type=MESH,
    ).start()

    for load in loads:
        load.wait()
    placing = pltpu.make_async_remote_copy(
        src_ref=placed.at[pl.ds(0, 63)], dst_ref=placed.at[pl.ds(0, 63)], send_sem=send_sem.at[2],
        recv_sem=recv_sem.at[2], device_id=(1 - side, grp), device_id_type=MESH,
    )
    placing.wait_recv()

    def scale(j, _):
        for h in range(4):
            columns = pl.ds(pl.multiple_of(j * 512 + h * LANES, LANES), LANES)
            for m in range(2):
                coef = placed[j, 1 + m, h:h + 1, :]
                keep = map_ref[m, j * 2 + h // 2]
                coef = jnp.where(keep != 0, coef, 0.0)
                part = pl.ds(m * rows, rows)
                held[part, columns] = held[part, columns] * jnp.broadcast_to(coef, (rows, LANES)).astype(BF16)
        return 0

    lax.fori_loop(0, groups, scale, 0)
    acc[...] = jnp.zeros_like(acc)

    answered = pltpu.make_async_remote_copy(
        src_ref=answers.at[pl.ds(0, 127)], dst_ref=answers.at[pl.ds(0, 127)], send_sem=send_sem.at[3],
        recv_sem=recv_sem.at[3], device_id=(1 - side, grp), device_id_type=MESH,
    )
    answered.wait_recv()

    table = answers[:, 0, :]
    shift_cols[pl.ds(0, LANES)] = jnp.broadcast_to(table[:, 0:1], (LANES, LANES))
    shift_cols[pl.ds(LANES, LANES)] = jnp.broadcast_to(table[:, 1:2], (LANES, LANES))

    def fill(i, cauchy):
        shift = shift_cols[...]
        for j in range(CHUNK // 512):
            for h in range(4):
                difference = placed[i * (CHUNK // 512) + j, 0, h:h + 1, :] - shift
                cauchy[:, pl.ds(j * 512 + h * LANES, LANES)] = pl.reciprocal(difference, approx=True).astype(BF16)

    def multiply(i, cauchy):
        columns = pl.ds(pl.multiple_of(i * CHUNK, CHUNK), CHUNK)
        acc[...] += lax.dot_general(
            held[:, columns], cauchy[...], (((1,), (1,)), ((), ())), preferred_element_type=F32
        )

    chunks = count // CHUNK
    fill(0, cauchy_a)

    def pair(i, _):
        fill(2 * i + 1, cauchy_b)
        multiply(2 * i, cauchy_a)
        fill((2 * i + 2) % chunks, cauchy_a)
        multiply(2 * i + 1, cauchy_b)
        return 0

    lax.fori_loop(0, chunks // 2, pair, 0)
    turned = table.T
    norm_u = jnp.concatenate([turned[2:3], turned[3:4]], axis=1)
    norm_v = jnp.concatenate([turned[4:5], turned[5:6]], axis=1)
    out_left[...] = (acc[pl.ds(0, rows)] * norm_u).astype(BF16)
    out_right[...] = (acc[pl.ds(rows, rows)] * norm_v).astype(BF16)
    out_offsets[...] = turned[6:8]
    gathered.wait_send()
    cross.wait_send()
    placing.wait_send()
    answered.wait_send()


def on_device(poles, coupling, kinds, permutation, block_map, left_vectors, right_vectors):
    rows, count = left_vectors.shape[1:]
    own = poles.shape[0] // LANES
    groups = lax.axis_size("grp")
    vmem = pl.BlockSpec(memory_space=pltpu.VMEM)
    anywhere = pl.BlockSpec(memory_space=pl.ANY)
    left, right, offsets = pl.pallas_call(
        merge_kernel,
        out_shape=(
            jax.ShapeDtypeStruct((rows, 2 * LANES), BF16),
            jax.ShapeDtypeStruct((rows, 2 * LANES), BF16),
            jax.ShapeDtypeStruct((2, LANES), F32),
        ),
        in_specs=[vmem, vmem, vmem, vmem, pl.BlockSpec(memory_space=pltpu.SMEM), anywhere, anywhere],
        out_specs=(vmem, vmem, vmem),
        scratch_shapes=[
            pltpu.VMEM((2 * rows, count), BF16),
            pltpu.VMEM((2, groups, 3, own, LANES), F32),
            pltpu.VMEM((LANES, count), BF16),
            pltpu.VMEM((count // LANES, 8, LANES), F32),
            pltpu.VMEM((32, count), BF16),
            pltpu.VMEM((32, LANES), F32),
            pltpu.VMEM((groups, 3, own, LANES), F32),
            pltpu.VMEM((groups, 8, LANES), F32),
            pltpu.VMEM((groups, 8, LANES), F32),
            pltpu.VMEM((2 * groups, 1, LANES), F32),
            pltpu.VMEM((2 * LANES, LANES), F32),
            pltpu.VMEM((2 * LANES, CHUNK), BF16),
            pltpu.VMEM((2 * LANES, CHUNK), BF16),
            pltpu.VMEM((2 * rows, 2 * LANES), F32),
            pltpu.SemaphoreType.DMA((2,)),
            pltpu.SemaphoreType.DMA((4,)),
            pltpu.SemaphoreType.DMA((4,)),
        ],
        compiler_params=pltpu.CompilerParams(
            collective_id=0, has_side_effects=True, vmem_limit_bytes=58 * 2**20
        ),
    )(
        poles.reshape(own, LANES),
        coupling.reshape(own, LANES),
        kinds.reshape(own, LANES),
        permutation.reshape(count // LANES, LANES),
        block_map[0, 0],
        left_vectors[0],
        right_vectors[0],
    )
    return left[None], right[None], offsets.reshape(2 * LANES)


def solution(mesh):
    return jax.shard_map(
        on_device,
        mesh=mesh,
        in_specs=(
            P(("side", "grp")),
            P(("side", "grp")),
            P(("side", "grp")),
            P("side", None),
            P("side", "grp", None, None),
            P("side", "grp", None),
            P("side", "grp", None),
        ),
        out_specs=(P("side", "grp", None), P("side", "grp", None), P()),
        check_vma=False,
    )
```

time: 1110 us -> 70.6 us (0.06); the launches traced: 1100 us -> 70.4 us
  blocking collectives: 638 us -> 0 us
  local copies, waits for them, and re-layouts: 298 us -> 4.26 us
  waiting for transfers between devices: 99.7 us -> 0 us
  Pallas kernels: 0 us -> 65.5 us
  matrix products: 41 us -> 0 us
  between operations: 14.4 us -> 0.64 us
    psum x10 -> x0, blocking collectives: 638 us -> none  [the longest x8 507 us: on_device(): sum_value, slope_value = lax.psum((own_value, own_slope), ('side', 'grp'))]
    scatter x2 -> x0, local copies, waits for them, and re-layouts: 294 us -> none  [the longest x1 147 us: on_device(): jnp.zeros((half_poles, root_total), jnp.bfloat16).at[placing].set(child_u)]
    all_gather x2 -> x0, waiting for transfers between devices: 98.9 us -> none  [the longest x1 98.9 us: on_device(): lax.all_gather(rows_v, 'grp', axis=0, tiled=True)]
    pallas_call x0 -> x1, Pallas kernels: none -> 65.5 us  [on_device(): pl.pallas_call(merge_kernel, out_shape=(jax.ShapeDtypeStruct((rows, 2 * L...]
    dot_general x2 -> x0, matrix products: 41 us -> none  [apply_blocks(): jnp.dot(vectors, placed * keep_mask[:, None], preferred_element_type=jnp....]
  transfers between devices with their start and end apart: 2 -> 0, of which waited for: 1 -> 0; matrix products, arithmetic and copies ran while one was open for 15% -> 0% of each run, Pallas kernels for 0% -> 0%
where the time goes in v1:
time: 70.6 us; the launch traced here: 70.4 us
  Pallas kernels  65.5 us (93%)
  local copies, waits for them, and re-layouts  4.26 us (6%)
    pallas_call x1, Pallas kernels, on_device(): pl.pallas_call(merge_kernel, out_shape=(jax.ShapeDtypeStruct((rows, 2 * L...  65.5 us
    unnamed x3, local copies, waits for them, and re-layouts  4.26 us

profile of v1, /device:TPU:1, one launch (start us, length us, event | category | flops | bytes accessed | tf_op | source)
XLA Modules:
  0.0 70.4 jit_solution(14381300136757914704)
XLA Ops:
  0.6 65.5 %shard_map.94 = (bf16[192,256]{1,0:T(8,128)(2,1)}, bf16[192,256]{1,0:T(8,128)(2,1)}, f32[2,128]{1,0:T(2,128)}) custom-call(f32[4,128]{1,0:T(4,128)} %bitcast.15, f32[4,128]{1,0:T(4,128)} %bitcast.16, s32[4,128]{1,0:T(4,128)} %bitcast.17, s32[256,128]{1,0:T(8,128)} %bitcast.12, s32[2,128]{1,0:T(2,128)} %bitcast.18, bf16[192,32768]{1,0:T(8,128)(2,1)} %bitcast.10, ...), custom_call_target="tpu_custom_call" | custom-call | tf_op jit(solution)/shard_map/pallas_call | solution.py:325
  66.2 1.5 %copy.13 = bf16[1,192,256]{2,1,0:T(8,128)(2,1)} copy(bf16[1,192,256]{2,1,0:T(8,128)(2,1)} %bitcast.14) | data formatting | bytes 196608
  67.7 1.5 %copy.14 = bf16[1,192,256]{2,1,0:T(8,128)(2,1)} copy(bf16[1,192,256]{2,1,0:T(8,128)(2,1)} %bitcast.13) | data formatting | bytes 196608
  69.2 1.2 %copy.15 = f32[256]{0:T(256)} copy(f32[256]{0:T(256)} %bitcast.19) | data formatting | bytes 2048

commit v2 on v1

--- a/solution.py
+++ b/solution.py
@@ -11,20 +11,22 @@
 ITERS = 8
 LANES = 128
 BW = 256
+LOW = 64
 CHUNK = 4096
+STRIP = 1024
 F32 = jnp.float32
 BF16 = jnp.bfloat16
 
 
-def far_first(i):
-    return (2 + i + i // 2 + 2 * (i // 3)) % 4
-
-
-def chip_at(grp, i):
-    x = (grp // 16 + far_first(i // 16)) % 4
-    y = (grp // 4 + far_first((i // 4) % 4)) % 4
-    z = (grp + far_first(i % 4)) % 4
-    return x * 16 + y * 4 + z
+def visit_chips(grp, act):
+    far_first = (2, 3, 1, 0)
+    x, rest = lax.div(grp, 16), lax.rem(grp, 16)
+    y, z = lax.div(rest, 4), lax.rem(rest, 4)
+    xs = [16 * lax.rem(x + far, 4) for far in far_first]
+    ys = [4 * lax.rem(y + far, 4) for far in far_first]
+    zs = [lax.rem(z + far, 4) for far in far_first]
+    for i in range(63):
+        act(xs[i // 16] + ys[i // 4 % 4] + zs[i % 4])
 
 
 def recip(value):
@@ -40,7 +42,7 @@
     poles_ref, coupling_ref, kinds_ref, perm_ref, map_ref, left_ref, right_ref,
     out_left, out_right, out_offsets,
     held, raw, one_hot, pieces, spread, found, placed, sq, weight, answers,
-    shift_cols, cauchy_a, cauchy_b, acc, load_sem, send_sem, recv_sem,
+    shift_cols, coefs, cauchy_a, cauchy_b, acc, load_sem, send_sem, recv_sem,
 ):
     side = lax.axis_index("side")
     grp = lax.axis_index("grp")
@@ -58,37 +60,34 @@
 
     barrier = pltpu.get_barrier_semaphore()
 
-    def greet(i, _):
-        other = (me + 1 + i) % 128
-        pl.semaphore_signal(barrier, inc=1, device_id=(other // 64, other % 64), device_id_type=MESH)
-        return 0
-
-    lax.fori_loop(0, 127, greet, 0)
+    def greet(chip, core):
+        pl.semaphore_signal(barrier, inc=1, device_id=(core, chip), device_id_type=MESH)
+
+    visit_chips(grp, lambda chip: greet(chip, side))
+    greet(grp, 1 - side)
 
     raw[side, grp, 0] = poles_ref[...]
     raw[side, grp, 1] = coupling_ref[...]
     raw[side, grp, 2] = kinds_ref[...].astype(F32)
-    low_digit = lax.broadcasted_iota(jnp.int32, (LANES, LANES), 0)
+    low_digit = lax.broadcasted_iota(jnp.int32, (LOW, LANES), 0)
 
     def mark(r, _):
-        own = perm_ref[pl.ds(r, 1), :] % LANES
+        own = perm_ref[pl.ds(r, 1), :] % LOW
         columns = pl.ds(pl.multiple_of(r * LANES, LANES), LANES)
         one_hot[:, columns] = jnp.where(own == low_digit, 1.0, 0.0).astype(BF16)
         return 0
 
     lax.fori_loop(0, count // LANES, mark, 0, unroll=4)
 
-    pl.semaphore_wait(barrier, 127)
-
-    def send_raw(i, _):
-        mine = raw.at[side, grp]
+    pl.semaphore_wait(barrier, 64)
+
+    def send(mine, k, chip, core):
         pltpu.make_async_remote_copy(
-            src_ref=mine, dst_ref=mine, send_sem=send_sem.at[0], recv_sem=recv_sem.at[0],
-            device_id=(side, chip_at(grp, i)), device_id_type=MESH,
+            src_ref=mine, dst_ref=mine, send_sem=send_sem.at[k], recv_sem=recv_sem.at[k],
+            device_id=(core, chip), device_id_type=MESH,
         ).start()
-        return 0
-
-    lax.fori_loop(0, 63, send_raw, 0)
+
+    visit_chips(grp, lambda chip: send(raw.at[side, grp], 0, chip, side))
     gathered = pltpu.make_async_remote_copy(
         src_ref=raw.at[0, pl.ds(0, 63)], dst_ref=raw.at[0, pl.ds(0, 63)], send_sem=send_sem.at[0],
         recv_sem=recv_sem.at[0], device_id=(1 - side, grp), device_id_type=MESH,
@@ -121,11 +120,11 @@
     lax.fori_loop(0, groups, split, 0, unroll=2)
 
     def mask(r, _):
-        digit = perm_ref[pl.ds(r, 1), :] // LANES - 4 * grp
+        digit = perm_ref[pl.ds(r, 1), :] // LOW - 8 * grp
         piece = pieces[r]
         columns = pl.ds(pl.multiple_of(r * LANES, LANES), LANES)
         spread[:, columns] = jnp.concatenate(
-            [jnp.where(digit == h, piece, 0.0) for h in range(4)], axis=0
+            [jnp.where(digit == h, piece, 0.0) for h in range(8)], axis=0
         ).astype(BF16)
         return 0
 
@@ -140,20 +139,15 @@
         return 0
 
     lax.fori_loop(0, count // CHUNK, look_up, 0)
-    digits = [found[pl.ds(q, 4, stride=8), :] for q in range(7)]
+    digits = [
+        jnp.concatenate([found[pl.ds(q + 8 * half, 4, stride=16), :] for half in range(2)], axis=1)
+        for q in range(7)
+    ]
     placed[grp, 0] = digits[0] + (digits[1] + digits[2])
     placed[grp, 1] = digits[3] + digits[4]
     placed[grp, 2] = digits[5] + digits[6]
 
-    def send_placed(i, _):
-        mine = placed.at[grp]
-        pltpu.make_async_remote_copy(
-            src_ref=mine, dst_ref=mine, send_sem=send_sem.at[2], recv_sem=recv_sem.at[2],
-            device_id=(side, chip_at(grp, i)), device_id_type=MESH,
-        ).start()
-        return 0
-
-    lax.fori_loop(0, 63, send_placed, 0)
+    visit_chips(grp, lambda chip: send(placed.at[grp], 2, chip, side))
 
     cross.wait_recv()
 
@@ -233,20 +227,12 @@
         row = jnp.where(lane == k, value, row)
     answers[me] = row
 
-    def send_answer(i, _):
-        mine = answers.at[me]
-        pltpu.make_async_remote_copy(
-            src_ref=mine, dst_ref=mine, send_sem=send_sem.at[3], recv_sem=recv_sem.at[3],
-            device_id=((side + i) % 2, chip_at(grp, i // 2)), device_id_type=MESH,
-        ).start()
-        return 0
-
-    lax.fori_loop(0, 126, send_answer, 0)
-    mine = answers.at[me]
-    pltpu.make_async_remote_copy(
-        src_ref=mine, dst_ref=mine, send_sem=send_sem.at[3], recv_sem=recv_sem.at[3],
-        device_id=(1 - side, grp), device_id_type=MESH,
-    ).start()
+    def send_answer(chip):
+        for core in (side, 1 - side):
+            send(answers.at[me], 3, chip, core)
+
+    visit_chips(grp, send_answer)
+    send(answers.at[me], 3, grp, 1 - side)
 
     for load in loads:
         load.wait()
@@ -256,18 +242,26 @@
     )
     placing.wait_recv()
 
-    def scale(j, _):
+    def spread_coefs(j, _):
         for h in range(4):
             columns = pl.ds(pl.multiple_of(j * 512 + h * LANES, LANES), LANES)
             for m in range(2):
-                coef = placed[j, 1 + m, h:h + 1, :]
-                keep = map_ref[m, j * 2 + h // 2]
-                coef = jnp.where(keep != 0, coef, 0.0)
-                part = pl.ds(m * rows, rows)
-                held[part, columns] = held[part, columns] * jnp.broadcast_to(coef, (rows, LANES)).astype(BF16)
-        return 0
-
-    lax.fori_loop(0, groups, scale, 0)
+                coef = jnp.where(map_ref[m, j * 2 + h // 2] != 0, placed[j, 1 + m, h:h + 1, :], 0.0)
+                coefs[m, :, columns] = jnp.broadcast_to(coef, (16, LANES)).astype(BF16)
+        return 0
+
+    lax.fori_loop(0, groups, spread_coefs, 0)
+
+    def scale(i, _):
+        columns = pl.ds(pl.multiple_of(i * STRIP, STRIP), STRIP)
+        for m in range(2):
+            coef = coefs[m, :, columns]
+            for t in range(rows // 16):
+                part = pl.ds(m * rows + t * 16, 16)
+                held[part, columns] = held[part, columns] * coef
+        return 0
+
+    lax.fori_loop(0, count // STRIP, scale, 0)
     acc[...] = jnp.zeros_like(acc)
 
     answered = pltpu.make_async_remote_copy(
@@ -314,6 +308,12 @@
     cross.wait_send()
     placing.wait_send()
     answered.wait_send()
+
+
+def hand_over(left_ref, right_ref, offsets_ref, out_left, out_right, out_offsets):
+    out_left[...] = left_ref[...]
+    out_right[...] = right_ref[...]
+    out_offsets[...] = offsets_ref[...]
 
 
 def on_device(poles, coupling, kinds, permutation, block_map, left_vectors, right_vectors):
@@ -334,15 +334,16 @@
         scratch_shapes=[
             pltpu.VMEM((2 * rows, count), BF16),
             pltpu.VMEM((2, groups, 3, own, LANES), F32),
-            pltpu.VMEM((LANES, count), BF16),
+            pltpu.VMEM((LOW, count), BF16),
             pltpu.VMEM((count // LANES, 8, LANES), F32),
-            pltpu.VMEM((32, count), BF16),
-            pltpu.VMEM((32, LANES), F32),
+            pltpu.VMEM((64, count), BF16),
+            pltpu.VMEM((64, LOW), F32),
             pltpu.VMEM((groups, 3, own, LANES), F32),
             pltpu.VMEM((groups, 8, LANES), F32),
             pltpu.VMEM((groups, 8, LANES), F32),
             pltpu.VMEM((2 * groups, 1, LANES), F32),
             pltpu.VMEM((2 * LANES, LANES), F32),
+            pltpu.VMEM((2, 16, count), BF16),
             pltpu.VMEM((2 * LANES, CHUNK), BF16),
             pltpu.VMEM((2 * LANES, CHUNK), BF16),
             pltpu.VMEM((2 * rows, 2 * LANES), F32),
@@ -362,6 +363,16 @@
         left_vectors[0],
         right_vectors[0],
     )
+    left, right, offsets = pl.pallas_call(
+        hand_over,
+        out_shape=(
+            jax.ShapeDtypeStruct(left.shape, BF16),
+            jax.ShapeDtypeStruct(right.shape, BF16),
+            jax.ShapeDtypeStruct(offsets.shape, F32),
+        ),
+        in_specs=[vmem] * 3,
+        out_specs=(vmem,) * 3,
+    )(left, right, offsets)
     return left[None], right[None], offsets.reshape(2 * LANES)
 
 

time: 70.6 us -> 46.1 us (0.65)
  Pallas kernels: 65.5 us -> 45 us
  local copies, waits for them, and re-layouts: 4.26 us -> 0 us
    pallas_call x1, Pallas kernels: 65.5 us -> 43.4 us  [on_device(): pl.pallas_call(merge_kernel, out_shape=(jax.ShapeDtypeStruct((rows, 2 * L...]
    unnamed x3 -> x0, local copies, waits for them, and re-layouts: 4.26 us -> none
    pallas_call x0 -> x1, Pallas kernels: none -> 1.63 us  [on_device(): pl.pallas_call(hand_over, out_shape=(jax.ShapeDtypeStruct(left.shape, BF1...]
where the time goes in v2:
time: 46.1 us; the launch traced here: 45.6 us
  Pallas kernels  45 us (98%)
  between operations  0.64 us (1%)
    pallas_call x1, Pallas kernels, on_device(): pl.pallas_call(merge_kernel, out_shape=(jax.ShapeDtypeStruct((rows, 2 * L...  43.4 us
    pallas_call x1, Pallas kernels, on_device(): pl.pallas_call(hand_over, out_shape=(jax.ShapeDtypeStruct(left.shape, BF1...  1.63 us

profile of v2, /device:TPU:1, one launch (start us, length us, event | category | flops | bytes accessed | tf_op | source)
XLA Modules:
  0.0 45.6 jit_solution(11145384987125307045)
XLA Ops:
  0.6 43.4 %shard_map.94 = (bf16[192,256]{1,0:T(8,128)(2,1)}, bf16[192,256]{1,0:T(8,128)(2,1)}, f32[2,128]{1,0:T(2,128)}) custom-call(f32[4,128]{1,0:T(4,128)} %bitcast.13, f32[4,128]{1,0:T(4,128)} %bitcast.14, s32[4,128]{1,0:T(4,128)} %bitcast.15, s32[256,128]{1,0:T(8,128)} %bitcast.12, s32[2,128]{1,0:T(2,128)} %bitcast.16, bf16[192,32768]{1,0:T(8,128)(2,1)} %bitcast.10, ...), custom_call_target="tpu_custom_call" | custom-call | tf_op jit(solution)/shard_map/pallas_call | solution.py:325
  44.0 1.6 %shard_map.95 = (bf16[192,256]{1,0:T(8,128)(2,1)}, bf16[192,256]{1,0:T(8,128)(2,1)}, f32[2,128]{1,0:T(2,128)}) custom-call(bf16[192,256]{1,0:T(8,128)(2,1)} %get-tuple-element.9.left_ref, bf16[192,256]{1,0:T(8,128)(2,1)} %get-tuple-element.10.right_ref, f32[2,128]{1,0:T(2,128)} %get-tuple-element.11.offsets_ref), custom_call_target="tpu_custom_call" | custom-call | tf_op jit(solution)/shard_map/pallas_call | solution.py:366

commit v3 on v2

--- a/solution.py
+++ b/solution.py
@@ -39,9 +39,9 @@
 
 
 def merge_kernel(
-    poles_ref, coupling_ref, kinds_ref, perm_ref, map_ref, left_ref, right_ref,
+    poles_ref, coupling_ref, kinds_hbm, perm_hbm, map_hbm, left_ref, right_ref,
     out_left, out_right, out_offsets,
-    held, raw, one_hot, pieces, spread, found, placed, sq, weight, answers,
+    perm_ref, kinds_ref, map_ref, held, raw, one_hot, pieces, spread, found, placed, sq, weight, answers,
     shift_cols, coefs, cauchy_a, cauchy_b, acc, load_sem, send_sem, recv_sem,
 ):
     side = lax.axis_index("side")
@@ -51,33 +51,43 @@
     count = left_ref.shape[1]
     groups = raw.shape[1]
 
+    barrier = pltpu.get_barrier_semaphore()
+
+    def greet(chip, core):
+        pl.semaphore_signal(barrier, inc=1, device_id=(core, chip), device_id_type=MESH)
+
+    visit_chips(grp, lambda chip: greet(chip, side))
+    greet(grp, 1 - side)
+
+    small = [
+        pltpu.make_async_copy(source, target, load_sem.at[2 + k])
+        for k, (source, target) in enumerate((
+            (perm_hbm, perm_ref), (poles_ref, raw.at[side, grp, 0]), (coupling_ref, raw.at[side, grp, 1]),
+            (kinds_hbm, kinds_ref), (map_hbm, map_ref),
+        ))
+    ]
     loads = [
         pltpu.make_async_copy(left_ref, held.at[pl.ds(0, rows)], load_sem.at[0]),
         pltpu.make_async_copy(right_ref, held.at[pl.ds(rows, rows)], load_sem.at[1]),
     ]
-    for load in loads:
+    for load in small + loads:
         load.start()
-
-    barrier = pltpu.get_barrier_semaphore()
-
-    def greet(chip, core):
-        pl.semaphore_signal(barrier, inc=1, device_id=(core, chip), device_id_type=MESH)
-
-    visit_chips(grp, lambda chip: greet(chip, side))
-    greet(grp, 1 - side)
-
-    raw[side, grp, 0] = poles_ref[...]
-    raw[side, grp, 1] = coupling_ref[...]
+    for load in small:
+        load.wait()
+
     raw[side, grp, 2] = kinds_ref[...].astype(F32)
     low_digit = lax.broadcasted_iota(jnp.int32, (LOW, LANES), 0)
+    high_digit = lax.broadcasted_iota(jnp.int32, (8, 8, LANES), 0).reshape(64, LANES) + 8 * grp
 
     def mark(r, _):
-        own = perm_ref[pl.ds(r, 1), :] % LOW
+        own = perm_ref[pl.ds(r, 1), :]
         columns = pl.ds(pl.multiple_of(r * LANES, LANES), LANES)
-        one_hot[:, columns] = jnp.where(own == low_digit, 1.0, 0.0).astype(BF16)
+        one_hot[:, columns] = jnp.where(own % LOW == low_digit, 1.0, 0.0).astype(BF16)
+        spread[:, columns] = jnp.where(own // LOW == high_digit, 1.0, 0.0).astype(BF16)
         return 0
 
     lax.fori_loop(0, count // LANES, mark, 0, unroll=4)
+    pieces[:, 7, :] = jnp.zeros_like(pieces[:, 7, :])
 
     pl.semaphore_wait(barrier, 64)
 
@@ -116,29 +126,18 @@
             pieces[pl.ds(j * 4, 4), q, :] = piece
         return 0
 
-    pieces[:, 7, :] = jnp.zeros_like(pieces[:, 7, :])
-    lax.fori_loop(0, groups, split, 0, unroll=2)
-
-    def mask(r, _):
-        digit = perm_ref[pl.ds(r, 1), :] // LOW - 8 * grp
-        piece = pieces[r]
-        columns = pl.ds(pl.multiple_of(r * LANES, LANES), LANES)
-        spread[:, columns] = jnp.concatenate(
-            [jnp.where(digit == h, piece, 0.0) for h in range(8)], axis=0
-        ).astype(BF16)
-        return 0
-
-    lax.fori_loop(0, count // LANES, mask, 0, unroll=4)
-    found[...] = jnp.zeros_like(found)
-
-    def look_up(i, _):
-        columns = pl.ds(pl.multiple_of(i * CHUNK, CHUNK), CHUNK)
-        found[...] += lax.dot_general(
-            spread[:, columns], one_hot[:, columns], (((1,), (1,)), ((), ())), preferred_element_type=F32
+    lax.fori_loop(0, groups, split, 0, unroll=8)
+    looked = None
+    for i in range(count // STRIP):
+        columns = pl.ds(i * STRIP, STRIP)
+        block = [pieces[i * (STRIP // LANES) + r] for r in range(STRIP // LANES)]
+        wide = jnp.concatenate([jnp.concatenate([p, p], axis=0).astype(BF16) for p in block], axis=1)
+        picked = jnp.concatenate([spread[pl.ds(16 * t, 16), columns] * wide for t in range(4)], axis=0)
+        part = lax.dot_general(
+            picked, one_hot[:, columns], (((1,), (1,)), ((), ())), preferred_element_type=F32
         )
-        return 0
-
-    lax.fori_loop(0, count // CHUNK, look_up, 0)
+        looked = part if looked is None else looked + part
+    found[...] = looked
     digits = [
         jnp.concatenate([found[pl.ds(q + 8 * half, 4, stride=16), :] for half in range(2)], axis=1)
         for q in range(7)
@@ -196,7 +195,9 @@
                     squared = inverse * inverse
                     sums[k][0] = sums[k][0] + jnp.sum(lead * squared, axis=0)
                     sums[k][1] = sums[k][1] + jnp.sum(tail * squared, axis=0)
-        return [[total(s) for s in pair] for pair in sums]
+        stack = jnp.concatenate([jnp.sum(s, axis=0, keepdims=True) for pair in sums for s in pair], axis=0)
+        stack = jnp.sum(stack, axis=1, keepdims=True)
+        return [[stack[2 * k + n:2 * k + n + 1] for n in range(2)] for k in range(2)]
 
     def step(_, shifts):
         sums = visit(shifts, lambda at, sq_block: (None, weight[at]))
@@ -329,9 +330,12 @@
             jax.ShapeDtypeStruct((rows, 2 * LANES), BF16),
             jax.ShapeDtypeStruct((2, LANES), F32),
         ),
-        in_specs=[vmem, vmem, vmem, vmem, pl.BlockSpec(memory_space=pltpu.SMEM), anywhere, anywhere],
+        in_specs=[anywhere] * 7,
         out_specs=(vmem, vmem, vmem),
         scratch_shapes=[
+            pltpu.VMEM((count // LANES, LANES), jnp.int32),
+            pltpu.VMEM((own, LANES), jnp.int32),
+            pltpu.SMEM(block_map.shape[2:], jnp.int32),
             pltpu.VMEM((2 * rows, count), BF16),
             pltpu.VMEM((2, groups, 3, own, LANES), F32),
             pltpu.VMEM((LOW, count), BF16),
@@ -347,7 +351,7 @@
             pltpu.VMEM((2 * LANES, CHUNK), BF16),
             pltpu.VMEM((2 * LANES, CHUNK), BF16),
             pltpu.VMEM((2 * rows, 2 * LANES), F32),
-            pltpu.SemaphoreType.DMA((2,)),
+            pltpu.SemaphoreType.DMA((7,)),
             pltpu.SemaphoreType.DMA((4,)),
             pltpu.SemaphoreType.DMA((4,)),
         ],

time: 46.1 us -> 42.1 us (0.913)
  Pallas kernels: 45 us -> 41.3 us
    pallas_call x1, Pallas kernels: 43.4 us -> 39.7 us  [on_device(): pl.pallas_call(merge_kernel, out_shape=(jax.ShapeDtypeStruct((rows, 2 * L...]
where the time goes in v3:
time: 42.1 us; the launch traced here: 41.9 us
  Pallas kernels  41.3 us (98%)
  between operations  0.64 us (2%)
    pallas_call x1, Pallas kernels, on_device(): pl.pallas_call(merge_kernel, out_shape=(jax.ShapeDtypeStruct((rows, 2 * L...  39.7 us
    pallas_call x1, Pallas kernels, on_device(): pl.pallas_call(hand_over, out_shape=(jax.ShapeDtypeStruct(left.shape, BF1...  1.63 us

profile of v3, /device:TPU:1, one launch (start us, length us, event | category | flops | bytes accessed | tf_op | source)
XLA Modules:
  0.0 41.9 jit_solution(14253420143426394428)
XLA Ops:
  0.6 39.7 %shard_map.94 = (bf16[192,256]{1,0:T(8,128)(2,1)}, bf16[192,256]{1,0:T(8,128)(2,1)}, f32[2,128]{1,0:T(2,128)}) custom-call(f32[4,128]{1,0:T(4,128)} %bitcast.13, f32[4,128]{1,0:T(4,128)} %bitcast.14, s32[4,128]{1,0:T(4,128)} %bitcast.15, s32[256,128]{1,0:T(8,128)} %bitcast.12, s32[2,128]{1,0:T(2,128)} %bitcast.16, bf16[192,32768]{1,0:T(8,128)(2,1)} %bitcast.10, ...), custom_call_target="tpu_custom_call" | custom-call | tf_op jit(solution)/shard_map/pallas_call | solution.py:326
  40.3 1.6 %shard_map.95 = (bf16[192,256]{1,0:T(8,128)(2,1)}, bf16[192,256]{1,0:T(8,128)(2,1)}, f32[2,128]{1,0:T(2,128)}) custom-call(bf16[192,256]{1,0:T(8,128)(2,1)} %get-tuple-element.9.left_ref, bf16[192,256]{1,0:T(8,128)(2,1)} %get-tuple-element.10.right_ref, f32[2,128]{1,0:T(2,128)} %get-tuple-element.11.offsets_ref), custom_call_target="tpu_custom_call" | custom-call | tf_op jit(solution)/shard_map/pallas_call | solution.py:370

commit v4 on v3

--- a/solution.py
+++ b/solution.py
@@ -14,6 +14,7 @@
 LOW = 64
 CHUNK = 4096
 STRIP = 1024
+WIDE = 2048
 F32 = jnp.float32
 BF16 = jnp.bfloat16
 
@@ -42,7 +43,7 @@
     poles_ref, coupling_ref, kinds_hbm, perm_hbm, map_hbm, left_ref, right_ref,
     out_left, out_right, out_offsets,
     perm_ref, kinds_ref, map_ref, held, raw, one_hot, pieces, spread, found, placed, sq, weight, answers,
-    shift_cols, coefs, cauchy_a, cauchy_b, acc, load_sem, send_sem, recv_sem,
+    shift_cols, cauchy_a, cauchy_b, acc, load_sem, send_sem, recv_sem,
 ):
     side = lax.axis_index("side")
     grp = lax.axis_index("grp")
@@ -243,26 +244,22 @@
     )
     placing.wait_recv()
 
-    def spread_coefs(j, _):
-        for h in range(4):
-            columns = pl.ds(pl.multiple_of(j * 512 + h * LANES, LANES), LANES)
-            for m in range(2):
-                coef = jnp.where(map_ref[m, j * 2 + h // 2] != 0, placed[j, 1 + m, h:h + 1, :], 0.0)
-                coefs[m, :, columns] = jnp.broadcast_to(coef, (16, LANES)).astype(BF16)
-        return 0
-
-    lax.fori_loop(0, groups, spread_coefs, 0)
-
     def scale(i, _):
-        columns = pl.ds(pl.multiple_of(i * STRIP, STRIP), STRIP)
+        columns = pl.ds(pl.multiple_of(i * WIDE, WIDE), WIDE)
         for m in range(2):
-            coef = coefs[m, :, columns]
+            line = []
+            for k in range(WIDE // BW):
+                keep = map_ref[m, i * (WIDE // BW) + k] != 0
+                for h in (2 * k, 2 * k + 1):
+                    coef = placed[i * (WIDE // 512) + h // 4, 1 + m, h % 4:h % 4 + 1, :]
+                    line.append(jnp.where(keep, coef, 0.0))
+            coef = jnp.broadcast_to(jnp.concatenate(line, axis=1), (16, WIDE)).astype(BF16)
             for t in range(rows // 16):
                 part = pl.ds(m * rows + t * 16, 16)
                 held[part, columns] = held[part, columns] * coef
         return 0
 
-    lax.fori_loop(0, count // STRIP, scale, 0)
+    lax.fori_loop(0, count // WIDE, scale, 0)
     acc[...] = jnp.zeros_like(acc)
 
     answered = pltpu.make_async_remote_copy(
@@ -347,7 +344,6 @@
             pltpu.VMEM((groups, 8, LANES), F32),
             pltpu.VMEM((2 * groups, 1, LANES), F32),
             pltpu.VMEM((2 * LANES, LANES), F32),
-            pltpu.VMEM((2, 16, count), BF16),
             pltpu.VMEM((2 * LANES, CHUNK), BF16),
             pltpu.VMEM((2 * LANES, CHUNK), BF16),
             pltpu.VMEM((2 * rows, 2 * LANES), F32),

time: 42.1 us -> 40.7 us (0.967)
  Pallas kernels: 41.3 us -> 39.9 us
    pallas_call x1, Pallas kernels: 39.7 us -> 38.3 us  [on_device(): pl.pallas_call(merge_kernel, out_shape=(jax.ShapeDtypeStruct((rows, 2 * L...]
where the time goes in v4:
time: 40.7 us; the launch traced here: 40.6 us
  Pallas kernels  39.9 us (98%)
  between operations  0.64 us (2%)
    pallas_call x1, Pallas kernels, on_device(): pl.pallas_call(merge_kernel, out_shape=(jax.ShapeDtypeStruct((rows, 2 * L...  38.3 us
    pallas_call x1, Pallas kernels, on_device(): pl.pallas_call(hand_over, out_shape=(jax.ShapeDtypeStruct(left.shape, BF1...  1.63 us

profile of v4, /device:TPU:1, one launch (start us, length us, event | category | flops | bytes accessed | tf_op | source)
XLA Modules:
  0.0 40.6 jit_solution(4915206146086296502)
XLA Ops:
  0.6 38.3 %shard_map.94 = (bf16[192,256]{1,0:T(8,128)(2,1)}, bf16[192,256]{1,0:T(8,128)(2,1)}, f32[2,128]{1,0:T(2,128)}) custom-call(f32[4,128]{1,0:T(4,128)} %bitcast.13, f32[4,128]{1,0:T(4,128)} %bitcast.14, s32[4,128]{1,0:T(4,128)} %bitcast.15, s32[256,128]{1,0:T(8,128)} %bitcast.12, s32[2,128]{1,0:T(2,128)} %bitcast.16, bf16[192,32768]{1,0:T(8,128)(2,1)} %bitcast.10, ...), custom_call_target="tpu_custom_call" | custom-call | tf_op jit(solution)/shard_map/pallas_call | solution.py:323
  39.0 1.6 %shard_map.95 = (bf16[192,256]{1,0:T(8,128)(2,1)}, bf16[192,256]{1,0:T(8,128)(2,1)}, f32[2,128]{1,0:T(2,128)}) custom-call(bf16[192,256]{1,0:T(8,128)(2,1)} %get-tuple-element.9.left_ref, bf16[192,256]{1,0:T(8,128)(2,1)} %get-tuple-element.10.right_ref, f32[2,128]{1,0:T(2,128)} %get-tuple-element.11.offsets_ref), custom_call_target="tpu_custom_call" | custom-call | tf_op jit(solution)/shard_map/pallas_call | solution.py:366

commit v5 on v4

--- a/solution.py
+++ b/solution.py
@@ -77,6 +77,17 @@
         load.wait()
 
     raw[side, grp, 2] = kinds_ref[...].astype(F32)
+
+    pl.semaphore_wait(barrier, 64)
+
+    def send(mine, k, chip, core):
+        pltpu.make_async_remote_copy(
+            src_ref=mine, dst_ref=mine, send_sem=send_sem.at[k], recv_sem=recv_sem.at[k],
+            device_id=(core, chip), device_id_type=MESH,
+        ).start()
+
+    visit_chips(grp, lambda chip: send(raw.at[side, grp], 0, chip, side))
+
     low_digit = lax.broadcasted_iota(jnp.int32, (LOW, LANES), 0)
     high_digit = lax.broadcasted_iota(jnp.int32, (8, 8, LANES), 0).reshape(64, LANES) + 8 * grp
 
@@ -90,15 +101,6 @@
     lax.fori_loop(0, count // LANES, mark, 0, unroll=4)
     pieces[:, 7, :] = jnp.zeros_like(pieces[:, 7, :])
 
-    pl.semaphore_wait(barrier, 64)
-
-    def send(mine, k, chip, core):
-        pltpu.make_async_remote_copy(
-            src_ref=mine, dst_ref=mine, send_sem=send_sem.at[k], recv_sem=recv_sem.at[k],
-            device_id=(core, chip), device_id_type=MESH,
-        ).start()
-
-    visit_chips(grp, lambda chip: send(raw.at[side, grp], 0, chip, side))
     gathered = pltpu.make_async_remote_copy(
         src_ref=raw.at[0, pl.ds(0, 63)], dst_ref=raw.at[0, pl.ds(0, 63)], send_sem=send_sem.at[0],
         recv_sem=recv_sem.at[0], device_id=(1 - side, grp), device_id_type=MESH,

time: 40.7 us -> 40.6 us (level)
  no operation moved by 1% of the time
where the time goes in v5:
time: 40.6 us; the launch traced here: 40.5 us
  Pallas kernels  39.9 us (98%)
  between operations  0.64 us (2%)
    pallas_call x1, Pallas kernels, on_device(): pl.pallas_call(merge_kernel, out_shape=(jax.ShapeDtypeStruct((rows, 2 * L...  38.2 us
    pallas_call x1, Pallas kernels, on_device(): pl.pallas_call(hand_over, out_shape=(jax.ShapeDtypeStruct(left.shape, BF1...  1.63 us

profile of v5, /device:TPU:1, one launch (start us, length us, event | category | flops | bytes accessed | tf_op | source)
XLA Modules:
  0.0 40.5 jit_solution(14613235563015212496)
XLA Ops:
  0.6 38.2 %shard_map.94 = (bf16[192,256]{1,0:T(8,128)(2,1)}, bf16[192,256]{1,0:T(8,128)(2,1)}, f32[2,128]{1,0:T(2,128)}) custom-call(f32[4,128]{1,0:T(4,128)} %bitcast.13, f32[4,128]{1,0:T(4,128)} %bitcast.14, s32[4,128]{1,0:T(4,128)} %bitcast.15, s32[256,128]{1,0:T(8,128)} %bitcast.12, s32[2,128]{1,0:T(2,128)} %bitcast.16, bf16[192,32768]{1,0:T(8,128)(2,1)} %bitcast.10, ...), custom_call_target="tpu_custom_call" | custom-call | tf_op jit(solution)/shard_map/pallas_call | solution.py:325
  38.9 1.6 %shard_map.95 = (bf16[192,256]{1,0:T(8,128)(2,1)}, bf16[192,256]{1,0:T(8,128)(2,1)}, f32[2,128]{1,0:T(2,128)}) custom-call(bf16[192,256]{1,0:T(8,128)(2,1)} %get-tuple-element.9.left_ref, bf16[192,256]{1,0:T(8,128)(2,1)} %get-tuple-element.10.right_ref, f32[2,128]{1,0:T(2,128)} %get-tuple-element.11.offsets_ref), custom_call_target="tpu_custom_call" | custom-call | tf_op jit(solution)/shard_map/pallas_call | solution.py:368
